TPU v7x, 128 devices: a whole 4x4x4 slice. The times are simulated.
128 devices in a mesh: row: 8 (over x_lo, z), col: 16 (over x_hi, y, core).
Axes of the slice: x: 4 (x_hi: 2, x_lo: 2; x = x_hi * 2 + x_lo), y: 4, z: 4, core: 2. Of those that a mesh axis runs over, the one named last changes fastest.
Arguments:
- inverse_block: float32 [12288, 12288], P('row', 'col'), may hold values from -0.14433757 to 0.14433757, as said below
- grid_position: int32 [12288], replicated, may hold values from 0 to 12287, each once
- panel_a: float32 [512, 12288], P('row', 'col'), may hold values from -1.5 to 1.5
- pivot_inverse_a: float32 [512, 512], replicated, may hold values from -6 to 6
- chosen_rows: int32 [8192], replicated, may hold values from 0 to 12287, as said below
- top_panel_b: float32 [512, 512], replicated, may hold values from -1.5 to 1.5
- panel_b: float32 [512, 8192], P('row', 'col'), may hold values from -1.5 to 1.5
- pivot_inverse_b: float32 [512, 512], replicated, may hold values from -6 to 6
Outputs:
- inverse_panel_a: float32 [12288, 512], P(('row', 'col'))
- diagonal_a: float32 [512, 512], replicated
- inverse_panel_b: float32 [12288, 512], P(('row', 'col'))
- inverse_top_b: float32 [512, 512], replicated
- diagonal_b: float32 [512, 512], replicated
Inputs may be any that keep to these rules, and one draw needn't show every extreme that they name: `grid_position`: each of 0 to 12287 appears once. `chosen_rows`: 8192 distinct values. `inverse_block`: symmetric: entry (i, j) equals entry (j, i) in grid storage order.
All inputs are finite; a program needn't handle non-finite values.
Results may differ from a plain program's by a relative error of at most 0.00008.
Values sent between devices are 32-bit elements; how exact they have to be, the bound alone decides.
A program may use at most 128 MiB of HBM per device.

v0:
```python
import jax
import jax.numpy as jnp
from jax import lax
from jax.sharding import PartitionSpec as P


def pick_columns(wide, index, limit):
    valid = (index < limit).astype(jnp.float32)
    taken = jnp.take(wide, jnp.minimum(index, limit - 1), axis=1)
    return taken * valid[None, :]


def select_columns(wide, source, start, length, limit):
    index = lax.dynamic_slice_in_dim(source, start, length, 0)
    return pick_columns(wide, index, limit)


def project(block, panel_t):
    return lax.dot_general(
        block,
        panel_t,
        (((1,), (1,)), ((), ())),
        precision=lax.Precision.HIGHEST,
        preferred_element_type=jnp.float32,
    )


def body(
    inverse_block,
    grid_position,
    panel_a,
    pivot_inverse_a,
    chosen_rows,
    top_panel_b,
    panel_b,
    pivot_inverse_b,
):
    exact = lax.Precision.HIGHEST
    rows_here = inverse_block.shape[0]
    cols_here = inverse_block.shape[1]
    order = grid_position.shape[0]
    count = chosen_rows.shape[0]
    row_count = lax.axis_size("row")
    own_rows = rows_here // lax.axis_size("col")
    col_start = lax.axis_index("col") * cols_here
    own_start = lax.axis_index("row") * rows_here + lax.axis_index("col") * own_rows
    group_starts = (
        jnp.arange(row_count, dtype=jnp.int32) * rows_here + lax.axis_index("col") * own_rows
    )
    group_index = (group_starts[:, None] + jnp.arange(own_rows, dtype=jnp.int32)[None, :]).reshape(
        -1
    )
    local_offset = lax.axis_index("row") * own_rows
    source_a = (
        jnp.zeros((order,), jnp.int32).at[grid_position].set(jnp.arange(order, dtype=jnp.int32))
    )
    source_b = (
        jnp.full((order,), count, jnp.int32)
        .at[grid_position[chosen_rows]]
        .set(jnp.arange(count, dtype=jnp.int32))
    )
    group_a = source_a[group_index]
    group_b = source_b[group_index]
    valid_own = (lax.dynamic_slice_in_dim(source_b, own_start, own_rows, 0) < count).astype(
        jnp.float32
    )
    wide_a = lax.all_gather(panel_a, "col", axis=1, tiled=True)
    cols_a, group_own_a = (
        lax.all_gather(
            select_columns(wide_a, source_a, col_start, cols_here, order), "row", axis=0, tiled=True
        ),
        lax.all_gather(pick_columns(wide_a, group_a, order), "row", axis=0, tiled=True),
    )
    product_a = lax.psum_scatter(
        project(inverse_block, cols_a), "col", scatter_dimension=0, tiled=True
    )
    wide_b = lax.all_gather(panel_b, "col", axis=1, tiled=True)
    cols_b, group_own_b = (
        lax.all_gather(
            select_columns(wide_b, source_b, col_start, cols_here, count), "row", axis=0, tiled=True
        ),
        lax.all_gather(pick_columns(wide_b, group_b, count), "row", axis=0, tiled=True),
    )
    product_b = lax.psum_scatter(
        project(inverse_block, cols_b), "col", scatter_dimension=0, tiled=True
    )
    own_a = lax.dynamic_slice_in_dim(group_own_a, local_offset, own_rows, 1)
    own_b = lax.dynamic_slice_in_dim(group_own_b, local_offset, own_rows, 1)
    inverse_panel_a = -product_a
    diag_part = jnp.dot(own_a, inverse_panel_a, precision=exact, preferred_element_type=jnp.float32)
    cross_part = lax.dot_general(
        inverse_panel_a,
        own_b,
        (((0,), (1,)), ((), ())),
        precision=exact,
        preferred_element_type=jnp.float32,
    )
    diag_total, cross = lax.psum((diag_part, cross_part), ("row", "col"))
    diagonal_a = pivot_inverse_a - diag_total
    inverse_top_b = -(
        jnp.dot(diagonal_a, top_panel_b, precision=exact, preferred_element_type=jnp.float32)
        + cross
    )
    bottom = product_b + jnp.dot(
        inverse_panel_a, top_panel_b, precision=exact, preferred_element_type=jnp.float32
    )
    inverse_panel_b = -bottom * valid_own[:, None]
    last_part = jnp.dot(own_b, inverse_panel_b, precision=exact, preferred_element_type=jnp.float32)
    last_total = lax.psum(last_part, ("row", "col"))
    diagonal_b = (
        pivot_inverse_b
        - jnp.dot(top_panel_b.T, inverse_top_b, precision=exact, preferred_element_type=jnp.float32)
        - last_total
    )
    return (inverse_panel_a, diagonal_a, inverse_panel_b, inverse_top_b, diagonal_b)


def solution(mesh):
    in_specs = (P("row", "col"), P(), P("row", "col"), P(), P(), P(), P("row", "col"), P())
    out_specs = (P(("row", "col"), None), P(), P(("row", "col"), None), P(), P())
    return jax.shard_map(body, mesh=mesh, in_specs=in_specs, out_specs=out_specs, check_vma=False)
```

profile of v0, /device:TPU:1, one launch (start us, length us, event | category | flops | bytes accessed | tf_op | source)
XLA Modules:
  0.0 630.5 jit_solution(11764547674448368654)
XLA Ops:
  7.2 0.0 all-gather.7.cloned.1.call-start
  7.2 1.9 copy.40
  9.2 0.0 all-gather.7.cloned.1.call-update
  9.2 0.0 all-gather.13.cloned.1.call-start
  9.2 1.7 copy.43
  11.0 0.0 all-gather.13.cloned.1.call-update
  11.0 0.0 all-gather.9.cloned.1.call-start
  11.1 0.8 compare_select_fusion.1
  11.9 45.4 %scatter_custom_fusion = s32[12288]{0:T(1024)S(1)} fusion(s32[12288]{0:T(1024)S(1)} %compare_select_fusion.1, s32[12288]{0:T(1024)S(1)} %iota.15, s32[]{:T(128)} %constant.4.clone.1), kind=kCustom, calls=%fused_computation.35 | custom fusion | bytes 49156 | tf_op jit(solution)/shard_map/scatter | solution.py:55
  57.3 0.1 compare_and_fusion.3
  57.4 21.3 %all-gather.7.cloned.1.call-done = f32[64,12288]{0,1:T(8,128)} async-done(((f32[64,768]{0,1:T(8,128)}), f32[64,12288]{0,1:T(8,128)}) %all-gather.7.cloned.1.call-update) | async-done | bytes 3145744 | tf_op jit(solution)/shard_map/all_gather | solution.py:67
  78.7 4.3 gather_fusion.3
  83.1 0.1 copy.41
  83.3 0.7 bitcast_multiply_fusion.3
  84.0 0.0 all-gather.9.cloned.1.call-update
  84.0 0.0 all-gather.15.cloned.1.call-start
  84.1 45.5 %gather_fusion.1 = s32[8192]{0:T(1024)S(1)} fusion(s32[12288]{0:T(1024)S(1)} %copy-done.1, s32[8192]{0:T(1024)S(1)} %fusion.11), kind=kCustom, calls=%fused_computation.5 | custom fusion | bytes 98304 | tf_op jit(solution)/shard_map/gather | solution.py:59
  129.7 30.5 %scatter_custom_fusion.1 = s32[12288]{0:T(1024)S(1)} fusion(s32[8192]{0:T(1024)S(1)} %bitcast.35, s32[8192]{0:T(1024)S(1)} %iota.17, s32[]{:T(128)} %constant.36.clone.1), kind=kCustom, calls=%fused_computation.33 | custom fusion | bytes 49156 | tf_op jit(solution)/shard_map/scatter | solution.py:60
  160.1 0.1 compare_and_fusion.1
  160.2 0.0 all-gather.13.cloned.1.call-done
  160.3 3.8 gather_fusion.5
  164.1 0.1 copy.44
  164.2 0.7 bitcast_multiply_fusion.1
  164.9 0.0 reduce-scatter.7.cloned.1.call-start
  165.0 4.1 all-gather.9.cloned.1.call-done
  169.1 11.3 %convolution_bitcast_fusion.1 = f32[1536,512]{0,1:T(8,128)} fusion(f32[512,768]{1,0:T(8,128)} %all-gather.9.cloned.1.call-done, f32[1536,768]{1,0:T(8,128)} %param.12), kind=kOutput, calls=%fused_computation.10 | convolution fusion | flops 7247757312 | bytes 9437184 | tf_op jit(solution)/shard_map/dot_general | solution.py:19
  180.3 3.7 copy.52
  184.0 0.0 all-gather.11.cloned.1.call-start
  184.1 0.1 iota_add_fusion
  184.2 0.1 add.114
  184.3 4.5 gather_fusion
  188.8 4.4 gather_fusion.4
  193.2 0.1 copy.42
  193.3 0.7 bitcast_multiply_fusion.2
  194.0 0.0 all-gather.17.cloned.1.call-start
  194.1 4.5 gather_fusion.2
  198.6 3.8 gather_fusion.6
  202.4 0.1 copy.46
  202.5 0.7 bitcast_multiply_fusion
  203.3 0.2 reduce-scatter.9.cloned.1.call-start
  203.5 7.6 %all-gather.15.cloned.1.call-done = f32[512,768]{1,0:T(8,128)} async-done(((f32[64,768]{1,0:T(8,128)}), f32[512,768]{1,0:T(8,128)}) %all-gather.15.cloned.1.call-update) | async-done | bytes 1572880 | tf_op jit(solution)/shard_map/all_gather | solution.py:79
  211.0 11.3 %convolution_bitcast_fusion = f32[1536,512]{0,1:T(8,128)} fusion(f32[512,768]{1,0:T(8,128)} %all-gather.15.cloned.1.call-done, f32[1536,768]{1,0:T(8,128)} %param.12), kind=kOutput, calls=%fused_computation.9 | convolution fusion | flops 7247757312 | bytes 9437184 | tf_op jit(solution)/shard_map/dot_general | solution.py:19
  222.4 3.5 copy.54
  225.9 0.0 all-reduce.3.cloned.1.call-start
  226.0 0.1 compare_convert_fusion.4
  226.0 68.4 %reduce-scatter.7.cloned.1.call-done = f32[96,512]{1,0:T(8,128)} async-done(((f32[1536,512]{1,0:T(8,128)}), f32[96,512]{1,0:T(8,128)}) %reduce-scatter.7.cloned.1.call-update) | async-done | bytes 196624
  294.4 1.0 copy.53
  295.5 35.6 %all-gather.11.cloned.1.call-done = f32[512,768]{1,0:T(8,128)} async-done(((f32[64,768]{1,0:T(8,128)}), f32[512,768]{1,0:T(8,128)}) %all-gather.11.cloned.1.call-update) | async-done | bytes 1572880 | tf_op jit(solution)/shard_map/all_gather | solution.py:72
  331.1 3.0 fusion.5
  334.1 39.1 %all-gather.17.cloned.1.call-done = f32[512,768]{1,0:T(8,128)} async-done(((f32[64,768]{1,0:T(8,128)}), f32[512,768]{1,0:T(8,128)}) %all-gather.17.cloned.1.call-update) | async-done | bytes 1572880 | tf_op jit(solution)/shard_map/all_gather | solution.py:82
  373.2 3.1 fusion.9
  376.3 80.5 %reduce-scatter.9.cloned.1.call-done = f32[96,512]{1,0:T(8,128)} async-done(((f32[1536,512]{1,0:T(8,128)}), f32[96,512]{1,0:T(8,128)}) %reduce-scatter.9.cloned.1.call-update) | async-done | bytes 196624 | tf_op jit(solution)/shard_map/reduce_scatter | solution.py:84
  456.8 1.7 fusion.4
  458.5 0.7 copy-done.7
  459.2 3.1 fusion.7
  462.3 1.6 copy.47
  464.0 0.7 neg.9
  464.7 1.8 copy.49
  466.5 149.7 %all-reduce.3.cloned.1.call-done = (f32[512,512]{1,0:T(8,128)}, f32[512,512]{1,0:T(8,128)}, f32[512,512]{0,1:T(8,128)}) async-done(((f32[512,512]{1,0:T(8,128)}, f32[512,512]{1,0:T(8,128)}, f32[512,512]{0,1:T(8,128)}), (f32[512,512]{1,0:T(8,128)}, f32[512,512]{1,0:T(8,128)}, f32[512,512]{0,1:T(8,128)})) %all-reduce.3.cloned.1.call-update) | async-done | bytes 3145744 | tf_op jit(solution)/shard_map/psum | solution.py:98
  616.2 1.6 sub.9
  617.8 1.9 fusion.2
  619.7 1.0 copy-done.3
  620.6 2.0 fusion.1
  622.6 1.3 copy.50
  (37 shorter events, 0.3 us)
Async XLA Ops:
  7.2 449.7 %copy-start = (f32[512,512]{1,0:T(8,128)S(1)}, f32[512,512]{1,0:T(8,128)}, u32[]{:S(2)}) copy-start(f32[512,512]{1,0:T(8,128)} %param.17) | copy-start | bytes 3145732
  7.2 76.9 %copy-start.1 = (s32[12288]{0:T(1024)S(1)}, s32[12288]{0:T(1024)}, u32[]{:S(2)}) copy-start(s32[12288]{0:T(1024)} %param.13) | copy-start | bytes 147460
  7.2 76.8 %copy-start.8 = (s32[8192]{0:T(1024)S(1)}, s32[8192]{0:T(1024)}, u32[]{:S(2)}) copy-start(s32[8192]{0:T(1024)} %param.16) | copy-start | bytes 98308
  7.2 71.5 %all-gather.7.cloned.1.call-start = ((), (), s32[]{:S(2)}) async-start(), calls=%async_computation.2 | async-start | bytes 6684672 | tf_op jit(solution)/shard_map/all_gather | solution.py:67
  9.2 151.1 %all-gather.13.cloned.1.call-start = ((), (), s32[]{:S(2)}) async-start(), calls=%async_computation.5 | async-start | bytes 4456448 | tf_op jit(solution)/shard_map/all_gather | solution.py:77
  11.0 158.0 %all-gather.9.cloned.1.call-start = ((), (), s32[]{:S(2)}) async-start(), calls=%async_computation.3 | async-start | bytes 1769472 | tf_op jit(solution)/shard_map/all_gather | solution.py:69
  84.0 127.1 %all-gather.15.cloned.1.call-start = ((), (), s32[]{:S(2)}) async-start(), calls=%async_computation.6 | async-start | bytes 1769472 | tf_op jit(solution)/shard_map/all_gather | solution.py:79
  164.9 129.5 %reduce-scatter.7.cloned.1.call-start = ((), (), s32[]{:S(2)}) async-start(), calls=%async_computation.8 | async-start | bytes 3342336
  184.0 147.1 %all-gather.11.cloned.1.call-start = ((), (), s32[]{:S(2)}) async-start(), calls=%async_computation.4 | async-start | bytes 1769472 | tf_op jit(solution)/shard_map/all_gather | solution.py:72
  194.0 179.2 %all-gather.17.cloned.1.call-start = ((), (), s32[]{:S(2)}) async-start(), calls=%async_computation.7 | async-start | bytes 1769472 | tf_op jit(solution)/shard_map/all_gather | solution.py:82
  203.3 253.6 %reduce-scatter.9.cloned.1.call-start = ((), (), s32[]{:S(2)}) async-start(), calls=%async_computation.9 | async-start | bytes 3342336 | tf_op jit(solution)/shard_map/reduce_scatter | solution.py:84
  225.9 390.3 %all-reduce.3.cloned.1.call-start = ((), (), s32[]{:S(2)}) async-start(), calls=%async_computation.10 | async-start | bytes 6291456 | tf_op jit(solution)/shard_map/psum | solution.py:98
  458.5 0.7 copy-start.7
  462.3 153.9 %copy-start.4 = (f32[512,512]{1,0:T(8,128)S(1)}, f32[512,512]{1,0:T(8,128)}, u32[]{:S(2)}) copy-start(f32[512,512]{1,0:T(8,128)} %param.15) | copy-start | bytes 3145732
  616.2 1.6 copy-start.6
  616.2 4.5 copy-start.5
  617.7 1.9 copy-start.2
  619.6 1.0 copy-start.3
Sparse Core Ops, SparseCore 0:
  11.1 67.6 all-gather.6
  81.8 53.0 all-gather.12
  137.1 31.9 all-gather.8
  171.1 39.8 all-gather.14
  214.9 79.4 reduce-scatter.6
  296.5 34.5 all-gather.10
  333.3 39.8 all-gather.16
  377.3 79.5 reduce-scatter.8
  462.5 153.5 all-reduce.2
where the time goes:
time: 631 us; the launch traced here: 630 us
  waiting for transfers between devices  406 us (64%)
  local copies, waits for them, and re-layouts  166 us (26%)
  matrix products  37.4 us (6%)
  between operations  14.2 us (2%)
  other arithmetic  6.35 us (1%)
    psum x1, waiting for transfers between devices, body(): diag_total, cross = lax.psum((diag_part, cross_part), ('row', 'col'))  150 us
    reduce_scatter x1, waiting for transfers between devices, body(): lax.psum_scatter(project(inverse_block, cols_b), 'col', scatter_dimension...  80.5 us
    unnamed x10, waiting for transfers between devices  68.6 us
    gather x1, local copies, waits for them, and re-layouts, body(): grid_position[chosen_rows]  45.5 us
    scatter x1, local copies, waits for them, and re-layouts, body(): jnp.zeros((order,), jnp.int32).at[grid_position]  45.4 us
    all_gather x1, waiting for transfers between devices, body(): lax.all_gather(pick_columns(wide_b, group_b, count), 'row', axis=0, tiled...  39.1 us
    all_gather x1, waiting for transfers between devices, body(): lax.all_gather(pick_columns(wide_a, group_a, order), 'row', axis=0, tiled...  35.6 us
    scatter x1, local copies, waits for them, and re-layouts, body(): source_b = jnp.full((order,), count, jnp.int32).at[grid_position[chosen_r...  30.5 us
  transfers between devices with their start and end apart: 9, of which 8 were waited for; matrix products, arithmetic and copies ran while one was open for 31% of the time, Pallas kernels for 0%

commit v1 on v0

--- a/solution.py
+++ b/solution.py
@@ -69,7 +69,15 @@
         lax.all_gather(
             select_columns(wide_a, source_a, col_start, cols_here, order), "row", axis=0, tiled=True
         ),
-        lax.all_gather(pick_columns(wide_a, group_a, order), "row", axis=0, tiled=True),
+        jnp.concatenate(
+            lax.all_to_all(
+                jnp.stack([pick_columns(wide_a, group_a, order)] * lax.axis_size("row")),
+                "row",
+                0,
+                0,
+            ),
+            axis=0,
+        ),
     )
     product_a = lax.psum_scatter(
         project(inverse_block, cols_a), "col", scatter_dimension=0, tiled=True

time: 631 us -> 594 us (0.941)
  waiting for transfers between devices: 406 us -> 364 us
    all_gather x1 -> x0, waiting for transfers between devices: 35.6 us -> none  [body(): lax.all_gather(pick_columns(wide_a, group_a, order), 'row', axis=0, tiled...]
    unnamed x10 -> x9, waiting for transfers between devices: 68.6 us -> 57.5 us
    all_gather x1, waiting for transfers between devices: 7.55 us -> 17.4 us  [body(): lax.all_gather(select_columns(wide_b, source_b, col_start, cols_here, cou...]
  transfers between devices with their start and end apart: 9 -> 9, of which waited for: 8 -> 7; matrix products, arithmetic and copies ran while one was open for 31% -> 33% of each run, Pallas kernels for 0% -> 0%
where the time goes in v1:
time: 594 us; the launch traced here: 593 us
  waiting for transfers between devices  364 us (61%)
  local copies, waits for them, and re-layouts  167 us (28%)
  matrix products  36.4 us (6%)
  between operations  14.5 us (2%)
    psum x1, waiting for transfers between devices, body(): diag_total, cross = lax.psum((diag_part, cross_part), ('row', 'col'))  150 us
    reduce_scatter x1, waiting for transfers between devices, body(): lax.psum_scatter(project(inverse_block, cols_b), 'col', scatter_dimension...  80.5 us
    unnamed x9, waiting for transfers between devices  57.5 us
    gather x1, local copies, waits for them, and re-layouts, body(): grid_position[chosen_rows]  45.5 us
    scatter x1, local copies, waits for them, and re-layouts, body(): jnp.zeros((order,), jnp.int32).at[grid_position]  45.4 us
    all_gather x1, waiting for transfers between devices, body(): lax.all_gather(pick_columns(wide_b, group_b, count), 'row', axis=0, tiled...  33.5 us
    scatter x1, local copies, waits for them, and re-layouts, body(): source_b = jnp.full((order,), count, jnp.int32).at[grid_position[chosen_r...  30.5 us
    dot_general x2, matrix products, project(): lax.dot_general(block, panel_t, (((1,), (1,)), ((), ())), precision=lax.P...  22.6 us
  transfers between devices with their start and end apart: 9, of which 7 were waited for; matrix products, arithmetic and copies ran while one was open for 33% of the time, Pallas kernels for 0%

profile of v1, /device:TPU:1, one launch (start us, length us, event | category | flops | bytes accessed | tf_op | source)
XLA Modules:
  0.0 592.9 jit_solution(11556661665047451897)
XLA Ops:
  7.2 0.0 all-gather.6.cloned.1.call-start
  7.2 1.9 copy.42
  9.2 0.0 all-gather.6.cloned.1.call-update
  9.2 0.0 all-gather.10.cloned.1.call-start
  9.2 1.7 copy.45
  11.0 0.0 all-gather.10.cloned.1.call-update
  11.0 0.0 all-gather.8.cloned.1.call-start
  11.1 0.8 compare_select_fusion.1
  11.9 45.4 %scatter_custom_fusion = s32[12288]{0:T(1024)S(1)} fusion(s32[12288]{0:T(1024)S(1)} %compare_select_fusion.1, s32[12288]{0:T(1024)S(1)} %iota.15, s32[]{:T(128)} %constant.4.clone.1), kind=kCustom, calls=%fused_computation.35 | custom fusion | bytes 49156 | tf_op jit(solution)/shard_map/scatter | solution.py:55
  57.3 0.1 compare_and_fusion.3
  57.4 21.3 %all-gather.6.cloned.1.call-done = f32[64,12288]{0,1:T(8,128)} async-done(((f32[64,768]{0,1:T(8,128)}), f32[64,12288]{0,1:T(8,128)}) %all-gather.6.cloned.1.call-update) | async-done | bytes 3145744 | tf_op jit(solution)/shard_map/all_gather | solution.py:67
  78.7 4.3 gather_fusion.3
  83.1 0.1 copy.43
  83.3 0.7 bitcast_multiply_fusion.3
  84.0 0.0 all-gather.8.cloned.1.call-update
  84.0 0.0 all-gather.12.cloned.1.call-start
  84.1 45.5 %gather_fusion.1 = s32[8192]{0:T(1024)S(1)} fusion(s32[12288]{0:T(1024)S(1)} %copy-done.1, s32[8192]{0:T(1024)S(1)} %fusion.11), kind=kCustom, calls=%fused_computation.5 | custom fusion | bytes 98304 | tf_op jit(solution)/shard_map/gather | solution.py:59
  129.7 30.5 %scatter_custom_fusion.1 = s32[12288]{0:T(1024)S(1)} fusion(s32[8192]{0:T(1024)S(1)} %bitcast.37, s32[8192]{0:T(1024)S(1)} %iota.17, s32[]{:T(128)} %constant.36.clone.1), kind=kCustom, calls=%fused_computation.33 | custom fusion | bytes 49156 | tf_op jit(solution)/shard_map/scatter | solution.py:60
  160.1 0.1 compare_and_fusion.1
  160.2 0.0 all-gather.10.cloned.1.call-done
  160.3 3.8 gather_fusion.5
  164.1 0.1 copy.46
  164.2 0.7 bitcast_multiply_fusion.1
  164.9 0.0 all-gather.12.cloned.1.call-update
  164.9 0.0 reduce-scatter.7.cloned.1.call-start
  165.0 4.1 all-gather.8.cloned.1.call-done
  169.1 11.3 %convolution_bitcast_fusion.1 = f32[1536,512]{0,1:T(8,128)} fusion(f32[512,768]{1,0:T(8,128)} %all-gather.8.cloned.1.call-done, f32[1536,768]{1,0:T(8,128)} %param.12), kind=kOutput, calls=%fused_computation.10 | convolution fusion | flops 7247757312 | bytes 9437184 | tf_op jit(solution)/shard_map/dot_general | solution.py:19
  180.4 3.7 copy.54
  184.0 0.0 all-gather.14.cloned.1.call-start
  184.1 0.1 iota_add_fusion
  184.2 0.1 add.114
  184.3 4.5 gather_fusion.2
  188.8 3.8 gather_fusion.6
  192.6 0.1 copy.48
  192.7 0.7 bitcast_multiply_fusion
  193.5 0.2 reduce-scatter.9.cloned.1.call-start
  193.7 17.4 %all-gather.12.cloned.1.call-done = f32[512,768]{1,0:T(8,128)} async-done(((f32[64,768]{1,0:T(8,128)}), f32[512,768]{1,0:T(8,128)}) %all-gather.12.cloned.1.call-update) | async-done | bytes 1572880 | tf_op jit(solution)/shard_map/all_gather | solution.py:87
  211.1 11.3 %convolution_bitcast_fusion = f32[1536,512]{0,1:T(8,128)} fusion(f32[512,768]{1,0:T(8,128)} %all-gather.12.cloned.1.call-done, f32[1536,768]{1,0:T(8,128)} %param.12), kind=kOutput, calls=%fused_computation.9 | convolution fusion | flops 7247757312 | bytes 9437184 | tf_op jit(solution)/shard_map/dot_general | solution.py:19
  222.4 3.6 copy.56
  226.0 4.5 gather_fusion
  230.5 4.6 gather_fusion.4
  235.1 0.1 copy.44
  235.3 1.3 stack.2
  236.6 4.4 all-to-all-start
  241.0 0.3 all-reduce.3.cloned.1.call-start
  241.3 0.1 compare_convert_fusion.4
  241.3 57.4 %reduce-scatter.7.cloned.1.call-done = f32[96,512]{1,0:T(8,128)} async-done(((f32[1536,512]{1,0:T(8,128)}), f32[96,512]{1,0:T(8,128)}) %reduce-scatter.7.cloned.1.call-update) | async-done | bytes 196624
  298.7 1.0 copy.55
  299.8 2.0 fusion.5
  301.8 33.5 %all-gather.14.cloned.1.call-done = f32[512,768]{1,0:T(8,128)} async-done(((f32[64,768]{1,0:T(8,128)}), f32[512,768]{1,0:T(8,128)}) %all-gather.14.cloned.1.call-update) | async-done | bytes 1572880 | tf_op jit(solution)/shard_map/all_gather | solution.py:90
  335.4 3.1 fusion.9
  338.5 80.5 %reduce-scatter.9.cloned.1.call-done = f32[96,512]{1,0:T(8,128)} async-done(((f32[1536,512]{1,0:T(8,128)}), f32[96,512]{1,0:T(8,128)}) %reduce-scatter.9.cloned.1.call-update) | async-done | bytes 196624 | tf_op jit(solution)/shard_map/reduce_scatter | solution.py:92
  419.0 1.7 fusion.4
  420.6 0.7 copy-done.7
  421.3 3.1 fusion.7
  424.5 1.6 copy.49
  426.1 0.7 neg.9
  426.8 1.8 copy.51
  428.6 149.7 %all-reduce.3.cloned.1.call-done = (f32[512,512]{1,0:T(8,128)}, f32[512,512]{1,0:T(8,128)}, f32[512,512]{0,1:T(8,128)}) async-done(((f32[512,512]{1,0:T(8,128)}, f32[512,512]{1,0:T(8,128)}, f32[512,512]{0,1:T(8,128)}), (f32[512,512]{1,0:T(8,128)}, f32[512,512]{1,0:T(8,128)}, f32[512,512]{0,1:T(8,128)})) %all-reduce.3.cloned.1.call-update) | async-done | bytes 3145744 | tf_op jit(solution)/shard_map/psum | solution.py:106
  578.3 1.6 sub.9
  579.9 1.9 fusion.2
  581.8 1.0 copy-done.3
  582.8 2.0 fusion.1
  584.8 1.3 copy.52
  (37 shorter events, 0.3 us)
Async XLA Ops:
  7.2 411.8 %copy-start = (f32[512,512]{1,0:T(8,128)S(1)}, f32[512,512]{1,0:T(8,128)}, u32[]{:S(2)}) copy-start(f32[512,512]{1,0:T(8,128)} %param.17) | copy-start | bytes 3145732
  7.2 76.9 %copy-start.1 = (s32[12288]{0:T(1024)S(1)}, s32[12288]{0:T(1024)}, u32[]{:S(2)}) copy-start(s32[12288]{0:T(1024)} %param.13) | copy-start | bytes 147460
  7.2 76.8 %copy-start.8 = (s32[8192]{0:T(1024)S(1)}, s32[8192]{0:T(1024)}, u32[]{:S(2)}) copy-start(s32[8192]{0:T(1024)} %param.16) | copy-start | bytes 98308
  7.2 71.5 %all-gather.6.cloned.1.call-start = ((), (), s32[]{:S(2)}) async-start(), calls=%async_computation.3 | async-start | bytes 6684672 | tf_op jit(solution)/shard_map/all_gather | solution.py:67
  9.2 151.1 %all-gather.10.cloned.1.call-start = ((), (), s32[]{:S(2)}) async-start(), calls=%async_computation.5 | async-start | bytes 4456448 | tf_op jit(solution)/shard_map/all_gather | solution.py:85
  11.0 158.0 %all-gather.8.cloned.1.call-start = ((), (), s32[]{:S(2)}) async-start(), calls=%async_computation.4 | async-start | bytes 1769472 | tf_op jit(solution)/shard_map/all_gather | solution.py:69
  84.0 127.1 %all-gather.12.cloned.1.call-start = ((), (), s32[]{:S(2)}) async-start(), calls=%async_computation.6 | async-start | bytes 1769472 | tf_op jit(solution)/shard_map/all_gather | solution.py:87
  164.9 133.8 %reduce-scatter.7.cloned.1.call-start = ((), (), s32[]{:S(2)}) async-start(), calls=%async_computation.8 | async-start | bytes 3342336
  184.0 151.3 %all-gather.14.cloned.1.call-start = ((), (), s32[]{:S(2)}) async-start(), calls=%async_computation.7 | async-start | bytes 1769472 | tf_op jit(solution)/shard_map/all_gather | solution.py:90
  193.5 225.5 %reduce-scatter.9.cloned.1.call-start = ((), (), s32[]{:S(2)}) async-start(), calls=%async_computation.9 | async-start | bytes 3342336 | tf_op jit(solution)/shard_map/reduce_scatter | solution.py:92
  236.6 63.2 %all-to-all-start = ((f32[8,64,768]{2,1,0:T(8,128)}), f32[8,64,768]{2,1,0:T(8,128)S(1)}, u32[]{:S(2)}, u32[]{:S(2)}) async-start(f32[8,64,768]{2,1,0:T(8,128)} %stack.2), calls=%async_computation | async-start | bytes 3145728 | tf_op jit(solution)/shard_map/all_to_all | solution.py:73
  241.0 337.3 %all-reduce.3.cloned.1.call-start = ((), (), s32[]{:S(2)}) async-start(), calls=%async_computation.10 | async-start | bytes 6291456 | tf_op jit(solution)/shard_map/psum | solution.py:106
  420.6 0.7 copy-start.7
  424.4 153.9 %copy-start.4 = (f32[512,512]{1,0:T(8,128)S(1)}, f32[512,512]{1,0:T(8,128)}, u32[]{:S(2)}) copy-start(f32[512,512]{1,0:T(8,128)} %param.15) | copy-start | bytes 3145732
  578.3 1.6 copy-start.6
  578.3 4.5 copy-start.5
  579.9 1.9 copy-start.2
  581.8 1.0 copy-start.3
Sparse Core Ops, SparseCore 0:
  11.1 67.6 all-gather.5
  81.8 53.0 all-gather.9
  137.1 31.9 all-gather.7
  171.1 39.8 all-gather.11
  215.0 83.7 reduce-scatter.6
  300.8 34.4 all-gather.13
  339.4 79.5 reduce-scatter.8
  424.6 153.6 all-reduce.2
